TPU v7x, 32 devices: a whole 2x2x4 slice. The times are simulated.
32 devices in a mesh: dp: 4 (over z), ctx: 2 (over x), shard: 4 (over y, core).
Axes of the slice: x: 2, y: 2, z: 4, core: 2. Of those that a mesh axis runs over, the one named last changes fastest.
Arguments:
- tokens: bfloat16 [8192, 1024], P(('dp', 'ctx', 'shard')), may hold values from -6 to 6
- cotangent: bfloat16 [8192, 1024], P(('dp', 'ctx', 'shard')), may hold values from -6 to 6
- picture_starts: int32 [4, 7], P('dp'), may hold values from 0 to 1792, as said below
- matrices: bfloat16 [1024, 12288], replicated
- vectors: bfloat16 [12, 1024], replicated
- master_matrices: float32 [1024, 12288], P(('dp', 'ctx', 'shard')), may hold values from -0.1875 to 0.1875
- master_vectors: float32 [12, 1024], P(None, ('dp', 'ctx', 'shard')), may hold values from -4 to 4
- first_matrices: float32 [1024, 12288], P(('dp', 'ctx', 'shard')), may hold values from -4 to 4
- first_vectors: float32 [12, 1024], P(None, ('dp', 'ctx', 'shard')), may hold values from -4 to 4
- second_matrices: float32 [1024, 12288], P(('dp', 'ctx', 'shard')), may hold values from 0.01 to 1
- second_vectors: float32 [12, 1024], P(None, ('dp', 'ctx', 'shard')), may hold values from 0.01 to 1
Outputs:
- layer_output: bfloat16 [8192, 1024], P(('dp', 'ctx', 'shard'))
- token_grads: float32 [8192, 1024], P(('dp', 'ctx', 'shard'))
- momentum_matrices: float32 [1024, 12288], P(('dp', 'ctx', 'shard'))
- momentum_vectors: float32 [12, 1024], P(None, ('dp', 'ctx', 'shard'))
- variance_matrices: float32 [1024, 12288], P(('dp', 'ctx', 'shard'))
- variance_vectors: float32 [12, 1024], P(None, ('dp', 'ctx', 'shard'))
- updated_matrices: float32 [1024, 12288], P(('dp', 'ctx', 'shard'))
- updated_vectors: float32 [12, 1024], P(None, ('dp', 'ctx', 'shard'))
- copied_matrices: bfloat16 [1024, 12288], P(('dp', 'ctx'))
- copied_vectors: bfloat16 [12, 1024], P(None, ('dp', 'ctx'))
Inputs may be any that keep to these rules, and one draw needn't show every extreme that they name: `picture_starts`: each sequence holds 7 picture blocks of 256 tokens given by their first positions in increasing order; blocks do not intersect and lie inside the sequence.
All inputs are finite; a program needn't handle non-finite values.
Results may differ from a plain program's by a relative error of at most 0.0095.
Values may be sent and summed in bfloat16 or wider, within the bound.
No kernel may reach another device: no remote copies, remote signals or barrier semaphores. Data moves between devices by JAX's collectives and lax.ppermute only.
A program may use at most 320 MiB of HBM per device.

v0:
```python
import math

import jax
import jax.numpy as jnp
from jax import lax
from jax.sharding import PartitionSpec as P

HEADS = 16
PIC = 256
STEP = 2


EPSILON = 1e-05
NEGATIVE = -1e30
BETA = 0.5
RATE = 0.03
DECAY_RATE = 0.1
ADAM_EPSILON = 1e-08


def token_tags(index, start_list, block_len):
    after = index[:, None] - start_list[None, :]
    inside = (after >= 0) & (after < block_len)
    offsets = jnp.sum(jnp.clip(after, 0, block_len - 1), axis=1)
    number = jnp.arange(1, start_list.shape[0] + 1, dtype=jnp.int32)
    picture = jnp.sum(jnp.where(inside, number[None, :], 0), axis=1) - 1
    return (index - offsets, picture)


def block_scores(query_heads, query_index, key_heads, key_index, start_list, slopes, factor):
    query_pos, query_pic = token_tags(query_index, start_list, PIC)
    key_pos, key_pic = token_tags(key_index, start_list, PIC)
    raw = jnp.einsum("qhd,khd->hqk", query_heads, key_heads, preferred_element_type=jnp.float32)
    distance = (query_pos[:, None] - key_pos[None, :]).astype(jnp.float32)
    logits = raw * factor - slopes[:, None, None] * distance[None, :, :]
    same = (query_pic[:, None] == key_pic[None, :]) & (query_pic[:, None] >= 0)
    visible = (key_index[None, :] <= query_index[:, None]) | same
    return (logits, visible[None, :, :])


def layer_norm(inputs):
    centered = inputs - jnp.mean(inputs, axis=1, keepdims=True)
    inverse_std = lax.rsqrt(jnp.mean(centered * centered, axis=1, keepdims=True) + EPSILON)
    return (centered * inverse_std, inverse_std)


def norm_backward(grad_normed, gain, normed, inverse_std):
    scaled = grad_normed * gain
    return inverse_std * (
        scaled
        - jnp.mean(scaled, axis=1, keepdims=True)
        - normed * jnp.mean(scaled * normed, axis=1, keepdims=True)
    )


def activate(value):
    return jax.nn.gelu(value, approximate=True)


def regroup(array, dim, outer, inner):
    shape = array.shape
    split = array.reshape(
        shape[:dim] + (outer, inner, shape[dim] // (outer * inner)) + shape[dim + 1 :]
    )
    return jnp.swapaxes(split, dim, dim + 1).reshape(shape)


def adam_update(master, first, second, gradient, correction, decay_rate):
    moment = BETA * first + (1.0 - BETA) * gradient
    variance = BETA * second + (1.0 - BETA) * gradient * gradient
    direction = moment / correction / (jnp.sqrt(variance / correction) + ADAM_EPSILON)
    return (moment, variance, master - RATE * (direction + decay_rate * master))


def shards(
    tokens,
    cotangent,
    picture_starts,
    matrices,
    vectors,
    master_matrices,
    master_vectors,
    first_matrices,
    first_vectors,
    second_matrices,
    second_vectors,
):
    row_count, model_width = tokens.shape
    ff_width = (matrices.shape[1] - 4 * model_width) // 2
    head_count = HEADS
    head_width = model_width // head_count
    factor = head_width ** (-0.5)
    group_size = lax.axis_size("ctx") * lax.axis_size("shard")
    group_rank = lax.axis_index("ctx") * lax.axis_size("shard") + lax.axis_index("shard")
    seq_length = row_count * group_size
    first_row = group_rank * row_count
    start_list = picture_starts[0]
    slopes = jnp.exp2(-8.0 * (jnp.arange(head_count, dtype=jnp.float32) + 1.0) / head_count)
    block_rows = math.gcd(seq_length, 512)
    block_count = seq_length // block_rows
    w_qkv = matrices[:, : 3 * model_width]
    w_proj = matrices[:, 3 * model_width : 4 * model_width]
    w_up = matrices[:, 4 * model_width : 4 * model_width + ff_width]
    w_down = matrices[:, 4 * model_width + ff_width :]
    inputs = tokens.astype(jnp.float32)
    vector_rows = vectors.astype(jnp.float32)
    up_bias = vector_rows[8:].reshape(ff_width)
    normed, inverse_std = layer_norm(inputs)
    hidden = (normed * vector_rows[0] + vector_rows[1]).astype(jnp.bfloat16)
    projected = jnp.dot(hidden, w_qkv, preferred_element_type=jnp.float32)
    queries = (projected[:, :model_width] + vector_rows[2]).astype(jnp.bfloat16)
    kv_bias = jnp.concatenate([jnp.zeros((model_width,), jnp.float32), vector_rows[3]])
    kv_local = (projected[:, model_width:] + kv_bias).astype(jnp.bfloat16)
    gathered = lax.all_gather(kv_local, ("ctx", "shard"), axis=0, tiled=True)
    query_index = first_row + jnp.arange(row_count, dtype=jnp.int32)
    query_heads = queries.reshape(row_count, head_count, head_width)

    def key_block(index):
        piece = lax.dynamic_slice_in_dim(gathered, index * block_rows, block_rows, 0)
        key_heads = piece[:, :model_width].reshape(block_rows, head_count, head_width)
        value_heads = piece[:, model_width:].reshape(block_rows, head_count, head_width)
        key_index = index * block_rows + jnp.arange(block_rows, dtype=jnp.int32)
        logits, visible = block_scores(
            query_heads, query_index, key_heads, key_index, start_list, slopes, factor
        )
        return (logits, visible, key_heads, value_heads)

    def running_total(index, carry):
        highest, total = carry
        logits, visible, key_heads, value_heads = key_block(index)
        masked = jnp.where(visible, logits, NEGATIVE)
        updated = jnp.maximum(highest, jnp.max(masked, axis=2))
        weights = jnp.where(visible, jnp.exp(logits - updated[:, :, None]), 0.0)
        return (updated, total * jnp.exp(highest - updated) + jnp.sum(weights, axis=2))

    start_high = jnp.full((head_count, row_count), NEGATIVE, jnp.float32)
    start_total = jnp.zeros((head_count, row_count), jnp.float32)
    highest, total = lax.fori_loop(0, block_count, running_total, (start_high, start_total))
    log_total = highest + jnp.log(total)

    def weighted_sum(index, accum):
        logits, visible, key_heads, value_heads = key_block(index)
        probs = jnp.where(visible, jnp.exp(logits - log_total[:, :, None]), 0.0).astype(
            jnp.bfloat16
        )
        return accum + jnp.einsum(
            "hqk,khd->qhd", probs, value_heads, preferred_element_type=jnp.float32
        )

    attended = lax.fori_loop(
        0, block_count, weighted_sum, jnp.zeros((row_count, head_count, head_width), jnp.float32)
    )
    attended_low = attended.reshape(row_count, model_width).astype(jnp.bfloat16)
    middle = (
        inputs + jnp.dot(attended_low, w_proj, preferred_element_type=jnp.float32) + vector_rows[4]
    )
    normed_two, inverse_two = layer_norm(middle)
    hidden_two = (normed_two * vector_rows[5] + vector_rows[6]).astype(jnp.bfloat16)
    pre_act = jnp.dot(hidden_two, w_up, preferred_element_type=jnp.float32) + up_bias
    act_low = activate(pre_act).astype(jnp.bfloat16)
    down_out = lax.dot_general(
        act_low, w_down, (((1,), (1,)), ((), ())), preferred_element_type=jnp.float32
    )
    layer_output = (middle + down_out + vector_rows[7]).astype(jnp.bfloat16)
    upstream = cotangent.astype(jnp.float32)
    grad_act = jnp.dot(cotangent, w_down, preferred_element_type=jnp.float32)
    gelu_value, gelu_pull = jax.vjp(activate, pre_act)
    grad_pre = gelu_pull(grad_act)[0].astype(jnp.bfloat16)
    grad_up_w = lax.dot_general(
        hidden_two, grad_pre, (((0,), (0,)), ((), ())), preferred_element_type=jnp.float32
    )
    grad_down_w = lax.dot_general(
        cotangent, act_low, (((0,), (0,)), ((), ())), preferred_element_type=jnp.float32
    )
    grad_two = lax.dot_general(
        grad_pre, w_up, (((1,), (1,)), ((), ())), preferred_element_type=jnp.float32
    )
    grad_mid = upstream + norm_backward(grad_two, vector_rows[5], normed_two, inverse_two)
    grad_mid_low = grad_mid.astype(jnp.bfloat16)
    grad_proj = lax.dot_general(
        attended_low, grad_mid_low, (((0,), (0,)), ((), ())), preferred_element_type=jnp.float32
    )
    grad_out = lax.dot_general(
        grad_mid_low, w_proj, (((1,), (1,)), ((), ())), preferred_element_type=jnp.float32
    ).astype(jnp.bfloat16)
    grad_heads = grad_out.reshape(row_count, head_count, head_width)
    delta = jnp.sum(grad_heads.astype(jnp.float32) * attended, axis=2).T

    def score_grads(index):
        logits, visible, key_heads, value_heads = key_block(index)
        probs = jnp.where(visible, jnp.exp(logits - log_total[:, :, None]), 0.0)
        product = jnp.einsum(
            "qhd,khd->hqk", grad_heads, value_heads, preferred_element_type=jnp.float32
        )
        grad_logits = (probs * (product - delta[:, :, None])).astype(jnp.bfloat16)
        return (probs, grad_logits, key_heads)

    def both_grads(index, carry):
        accum, key_terms = carry
        probs, grad_logits, key_heads = score_grads(index)
        accum = (
            accum
            + jnp.einsum("hqk,khd->qhd", grad_logits, key_heads, preferred_element_type=jnp.float32)
            * factor
        )
        grad_key = (
            jnp.einsum("hqk,qhd->khd", grad_logits, query_heads, preferred_element_type=jnp.float32)
            * factor
        )
        grad_value = jnp.einsum(
            "hqk,qhd->khd",
            probs.astype(jnp.bfloat16),
            grad_heads,
            preferred_element_type=jnp.float32,
        )
        term = jnp.concatenate(
            [
                grad_key.reshape(block_rows, model_width),
                grad_value.reshape(block_rows, model_width),
            ],
            axis=1,
        )
        return (accum, lax.dynamic_update_slice_in_dim(key_terms, term, index * block_rows, 0))

    grad_query, key_terms = lax.fori_loop(
        0,
        block_count,
        both_grads,
        (
            jnp.zeros((row_count, head_count, head_width), jnp.float32),
            jnp.zeros((seq_length, 2 * model_width), jnp.float32),
        ),
    )
    own_key_grads = lax.psum_scatter(key_terms, ("ctx", "shard"), scatter_dimension=0, tiled=True)
    grad_qkv = jnp.concatenate(
        [grad_query.reshape(row_count, model_width), own_key_grads], axis=1
    ).astype(jnp.bfloat16)
    grad_qkv_weights = lax.dot_general(
        hidden, grad_qkv, (((0,), (0,)), ((), ())), preferred_element_type=jnp.float32
    )
    grad_hidden = lax.dot_general(
        grad_qkv, w_qkv, (((1,), (1,)), ((), ())), preferred_element_type=jnp.float32
    )
    query_bias_grad = jnp.sum(grad_qkv[:, :model_width].astype(jnp.float32), axis=0)
    value_bias_grad = jnp.sum(grad_qkv[:, 2 * model_width :].astype(jnp.float32), axis=0)
    grad_vectors = jnp.concatenate(
        [
            jnp.stack(
                [
                    jnp.sum(grad_hidden * normed, axis=0),
                    jnp.sum(grad_hidden, axis=0),
                    query_bias_grad,
                    value_bias_grad,
                    jnp.sum(grad_mid, axis=0),
                    jnp.sum(grad_two * normed_two, axis=0),
                    jnp.sum(grad_two, axis=0),
                    jnp.sum(upstream, axis=0),
                ]
            ),
            jnp.sum(grad_pre.astype(jnp.float32), axis=0).reshape(
                ff_width // model_width, model_width
            ),
        ],
        axis=0,
    )
    token_grads = grad_mid + norm_backward(grad_hidden, vector_rows[0], normed, inverse_std)
    grad_matrix = jnp.concatenate([grad_qkv_weights, grad_proj, grad_up_w, grad_down_w], axis=1)
    shard_count = lax.axis_size("shard")
    replicas = lax.axis_size("dp") * lax.axis_size("ctx")
    part_matrix, part_vec = (
        lax.psum_scatter(
            regroup(grad_matrix, 0, replicas, shard_count), "shard", scatter_dimension=0, tiled=True
        ),
        lax.psum_scatter(
            regroup(grad_vectors, 1, replicas, shard_count),
            "shard",
            scatter_dimension=1,
            tiled=True,
        ),
    )
    part_matrix, part_vec = (
        lax.psum_scatter(part_matrix, ("dp", "ctx"), scatter_dimension=0, tiled=True),
        lax.psum_scatter(part_vec, ("dp", "ctx"), scatter_dimension=1, tiled=True),
    )
    root = (row_count * lax.axis_size("dp") * group_size) ** (-0.5)
    correction = 1.0 - BETA**STEP
    moment_w, variance_w, updated_w = adam_update(
        master_matrices, first_matrices, second_matrices, part_matrix * root, correction, DECAY_RATE
    )
    moment_v, variance_v, updated_v = adam_update(
        master_vectors, first_vectors, second_vectors, part_vec * root, correction, 0.0
    )
    copied_w, copied_v = (
        lax.all_gather(updated_w.astype(jnp.bfloat16), "shard", axis=0, tiled=True),
        lax.all_gather(updated_v.astype(jnp.bfloat16), "shard", axis=1, tiled=True),
    )
    return (
        layer_output,
        token_grads,
        moment_w,
        moment_v,
        variance_w,
        variance_v,
        updated_w,
        updated_v,
        copied_w,
        copied_v,
    )


def solution(mesh):
    in_specs = (
        P(("dp", "ctx", "shard"), None),
        P(("dp", "ctx", "shard"), None),
        P("dp", None),
        P(),
        P(),
        P(("dp", "ctx", "shard"), None),
        P(None, ("dp", "ctx", "shard")),
        P(("dp", "ctx", "shard"), None),
        P(None, ("dp", "ctx", "shard")),
        P(("dp", "ctx", "shard"), None),
        P(None, ("dp", "ctx", "shard")),
    )
    out_specs = (
        P(("dp", "ctx", "shard"), None),
        P(("dp", "ctx", "shard"), None),
        P(("dp", "ctx", "shard"), None),
        P(None, ("dp", "ctx", "shard")),
        P(("dp", "ctx", "shard"), None),
        P(None, ("dp", "ctx", "shard")),
        P(("dp", "ctx", "shard"), None),
        P(None, ("dp", "ctx", "shard")),
        P(("dp", "ctx"), None),
        P(None, ("dp", "ctx")),
    )
    return jax.shard_map(shards, mesh=mesh, in_specs=in_specs, out_specs=out_specs, check_vma=False)
```

profile of v0, /device:TPU:0, one launch (start us, length us, event | category | flops | bytes accessed | tf_op | source)
XLA Modules:
  0.0 1129.0 jit_solution(9749407350568820883)
XLA Ops:
  21.1 55.4 %all-gather.4.cloned.1.call-done = bf16[2048,2048]{1,0:T(8,128)(2,1)} async-done(((bf16[256,2048]{1,0:T(8,128)(2,1)}), bf16[2048,2048]{1,0:T(8,128)(2,1)}) %all-gather.4.cloned.1.call-update) | async-done | bytes 8388624 | tf_op jit(solution)/shard_map/all_gather | solution.py:114
  76.4 12.3 %copy.95 = bf16[2048,2048]{0,1:T(8,128)(2,1)} copy(bf16[2048,2048]{1,0:T(8,128)(2,1)} %all-gather.4.cloned.1.call-done) | data formatting | bytes 16777216
  88.8 28.4 %while.55 = (s32[]{:T(128)}, f32[16,256]{1,0:T(8,128)S(1)}, f32[16,256]{1,0:T(8,128)S(1)}, s32[1,7]{1,0:T(1,128)S(1)}, bf16[2048,2048]{0,1:T(8,128)(2,1)}, /*ind...) while((s32[]{:T(128)}, f32[16,256]{1,0:T(8,128)S(1)}, ...), condition=%wide.region_9.10_spmd.clone, body=%wide.region_2.9_spmd.clone.sunk | while | flops 292356128 | bytes 22662156 | solution.py:138
  117.2 38.9 %while.56 = (s32[]{:T(128)}, f32[256,16,64]{0,2,1:T(8,128)}, bf16[2048,2048]{0,1:T(8,128)(2,1)}, s32[1,7]{1,0:T(1,128)S(1)}, bf16[256,16,64]{0,2,1:T(8,128)(2,1)...) while((s32[]{:T(128)}, f32[256,16,64]{0,2,1:T(8,128)}, ...), condition=%wide.region_15.16_spmd.clone, body=%wide.region_10.15_spmd.clone.sunk | while | flops 550809664 | bytes 10275813 | solution.py:150
  130.7 5.7 fusion.185
  160.3 5.9 fusion.71
  166.2 9.1 convert_reduce_fusion
  175.2 6.5 multiply_reduce_fusion
  190.5 7.8 broadcast_in_dim.365
  198.4 57.2 %while.57 = (s32[]{:T(128)}, f32[256,16,64]{0,2,1:T(8,128)S(1)}, f32[2048,2048]{0,1:T(8,128)}, bf16[2048,2048]{0,1:T(8,128)(2,1)}, s32[1,7]{1,0:T(1,128)S(1)}, /...) while((s32[]{:T(128)}, f32[256,16,64]{0,2,1:T(8,128)S(1)}, ...), condition=%wide.region_26.27_spmd.clone, body=%wide.region_21.26_spmd.clone.sunk | while | flops 1374728192 | bytes 66014300 | solution.py:225
  260.6 11.6 %fusion.128 = f32[1024,4096]{1,0:T(8,128)} fusion(bf16[256,4096]{1,0:T(8,128)(2,1)S(1)} %copy-done.13, f32[256,1024]{1,0:T(8,128)S(1)} %get-tuple-element.1097, f32[1024]{0:T(1024)S(1)} %bitcast.211, f32[1024]{0:T(1024)S(1)} %bitcast.208, f32[256]{0:T(256)S(1)} %add_rsqrt_fusion, f32[256]{0:T(256)S(1)} %broadcast_multiply_fusion.4), kind=kOutput, calls=%fused_computation.213 | convolution fusion | flops 2148794368 | bytes 19933184 | tf_op jit(solution)/shard_map/dot_general | solution.py:169
  272.2 10.9 convolution_bitcast_fusion
  283.2 88.6 %reduce-scatter.8.cloned.1.call-done = f32[256,2048]{0,1:T(8,128)} async-done(((f32[2048,2048]{0,1:T(8,128)}), f32[256,2048]{0,1:T(8,128)}) %reduce-scatter.8.cloned.1.call-update) | async-done | bytes 2097168 | tf_op jit(solution)/shard_map/reduce_scatter | solution.py:234
  373.5 7.6 fusion.120
  381.0 33.2 %pad_maximum_fusion = f32[1024,12288]{1,0:T(8,128)} fusion(f32[1024,4096]{1,0:T(8,128)} %convolution_bitcast_fusion, f32[1024,4096]{1,0:T(8,128)} %fusion.128, f32[1024,1024]{1,0:T(8,128)} %fusion.121, f32[1024,3072]{1,0:T(8,128)} %fusion.120), kind=kLoop, calls=%fused_computation.111 | loop fusion | flops 37748736 | bytes 100663296 | tf_op jit(solution)/shard_map/concatenate | solution.py:267
  414.2 34.3 %copy.100 = f32[4,8,32,12288]{3,2,1,0:T(8,128)} copy(f32[4,8,32,12288]{3,2,0,1:T(8,128)} %bitcast.186) | data formatting | bytes 100663296 | tf_op jit(solution)/shard_map/transpose | solution.py:65
  450.1 5.8 fusion.117
  457.0 335.0 %reduce-scatter.10.cloned.1.call-done = f32[256,12288]{1,0:T(8,128)} async-done(((f32[1024,12288]{1,0:T(8,128)}), f32[256,12288]{1,0:T(8,128)}) %reduce-scatter.10.cloned.1.call-update) | async-done | bytes 12582928 | tf_op jit(solution)/shard_map/reduce_scatter | solution.py:271
  792.0 22.4 %reduce-scatter.14.cloned.1.call-done = f32[12,256]{1,0:T(8,128)} async-done(((f32[12,1024]{1,0:T(8,128)}), f32[12,256]{1,0:T(8,128)}) %reduce-scatter.14.cloned.1.call-update) | async-done | bytes 12304 | tf_op jit(solution)/shard_map/reduce_scatter | solution.py:274
  816.1 209.1 %reduce-scatter.12.cloned.1.call-done = f32[32,12288]{1,0:T(8,128)} async-done(((f32[256,12288]{1,0:T(8,128)}), f32[32,12288]{1,0:T(8,128)}) %reduce-scatter.12.cloned.1.call-update) | async-done | bytes 1572880 | tf_op jit(solution)/shard_map/reduce_scatter | solution.py:282
  1025.2 6.1 fusion.129
  1031.4 8.4 fusion.99
  1041.2 47.1 %reduce-scatter.16.cloned.1.call-done = f32[32,12]{1,0:T(8,128)} async-done(((f32[256,12]{1,0:T(8,128)}), f32[32,12]{1,0:T(8,128)}) %reduce-scatter.16.cloned.1.call-update) | async-done | bytes 1552
  1095.6 22.5 %all-gather.6.cloned.1.call-done = bf16[128,12288]{1,0:T(8,128)(2,1)} async-done(((bf16[32,12288]{1,0:T(8,128)(2,1)}), bf16[128,12288]{1,0:T(8,128)(2,1)}) %all-gather.6.cloned.1.call-update) | async-done | bytes 3145744 | tf_op jit(solution)/shard_map/all_gather | solution.py:294
  (341 shorter events, 168.1 us)
Async XLA Ops:
  7.2 69.3 %all-gather.4.cloned.1.call-start = ((), (), s32[]{:S(2)}) async-start(), calls=%async_computation.5 | async-start | bytes 9437184 | tf_op jit(solution)/shard_map/all_gather | solution.py:114
  8.4 7.9 copy-start.21
  9.8 6.5 copy-start.23
  19.2 352.5 %reduce-scatter.8.cloned.1.call-start = ((), (), s32[]{:S(2)}) async-start(), calls=%async_computation.6 | async-start | bytes 18874368 | tf_op jit(solution)/shard_map/reduce_scatter | solution.py:234
  21.1 67.7 %copy-start.15 = (s32[1,7]{1,0:T(1,128)S(1)}, s32[1,7]{1,0:T(1,128)}, u32[]{:S(2)}) copy-start(s32[1,7]{1,0:T(1,128)} %param.19) | copy-start | bytes 88
  117.2 40.2 %copy-start = (bf16[256,1024]{1,0:T(8,128)(2,1)S(1)}, bf16[256,1024]{1,0:T(8,128)(2,1)}, u32[]{:S(2)}) copy-start(bf16[256,1024]{1,0:T(8,128)(2,1)} %param.17) | copy-start | bytes 1572868
  166.2 9.1 copy-start.4
  255.6 536.3 %reduce-scatter.10.cloned.1.call-start = ((), (), s32[]{:S(2)}) async-start(), calls=%async_computation.7 | async-start | bytes 62914560 | tf_op jit(solution)/shard_map/reduce_scatter | solution.py:271
  260.6 11.6 %copy-start.5 = (f32[256,4096]{1,0:T(8,128)S(1)}, f32[256,4096]{1,0:T(8,128)}, u32[]{:S(2)}) copy-start(f32[256,4096]{1,0:T(8,128)} %copy-done.4) | copy-start | bytes 12582916
  272.2 101.2 %copy-start.1 = (bf16[256,1024]{1,0:T(8,128)(2,1)S(1)}, bf16[256,1024]{1,0:T(8,128)(2,1)}, u32[]{:S(2)}) copy-start(bf16[256,1024]{1,0:T(8,128)(2,1)} %param.17) | copy-start | bytes 1572868
  272.2 101.2 %copy-start.17 = (f32[1,1024]{1,0:T(1,128)S(1)}, f32[1,1024]{1,0:T(1,128)}, u32[]{:S(2)}) copy-start(f32[1,1024]{1,0:T(1,128)} %copy-done.16) | copy-start | bytes 12292
  272.2 101.2 %copy-start.20 = (f32[1,1024]{1,0:T(1,128)S(1)}, f32[1,1024]{1,0:T(1,128)}, u32[]{:S(2)}) copy-start(f32[1,1024]{1,0:T(1,128)} %copy-done.19) | copy-start | bytes 12292
  272.2 101.2 %copy-start.22 = (f32[256]{0:T(256)S(1)}, f32[256]{0:T(256)}, u32[]{:S(2)}) copy-start(f32[256]{0:T(256)} %copy-done.21) | copy-start | bytes 3076
  272.2 101.2 %copy-start.24 = (f32[256]{0:T(256)S(1)}, f32[256]{0:T(256)}, u32[]{:S(2)}) copy-start(f32[256]{0:T(256)} %copy-done.23) | copy-start | bytes 3076
  448.6 365.8 %reduce-scatter.14.cloned.1.call-start = ((), (), s32[]{:S(2)}) async-start(), calls=%async_computation.9 | async-start | bytes 81920 | tf_op jit(solution)/shard_map/reduce_scatter | solution.py:274
  456.9 568.3 %reduce-scatter.12.cloned.1.call-start = ((), (), s32[]{:S(2)}) async-start(), calls=%async_computation.8 | async-start | bytes 14155776 | tf_op jit(solution)/shard_map/reduce_scatter | solution.py:282
  792.0 296.3 %reduce-scatter.16.cloned.1.call-start = ((), (), s32[]{:S(2)}) async-start(), calls=%async_computation.11 | async-start | bytes 147456
  815.9 215.5 %copy-start.31 = (f32[1,1024]{1,0:T(1,128)S(1)}, f32[1,1024]{1,0:T(1,128)}, u32[]{:S(2)}) copy-start(f32[1,1024]{1,0:T(1,128)} %get-tuple-element.1090) | copy-start | bytes 12292
  815.9 302.2 %all-gather.6.cloned.1.call-start = ((), (), s32[]{:S(2)}) async-start(), calls=%async_computation.10 | async-start | bytes 3932160 | tf_op jit(solution)/shard_map/all_gather | solution.py:294
  1031.4 8.4 copy-start.3
  1031.4 8.4 copy-start.14
  1031.4 57.7 %copy-start.28 = (f32[12,32]{1,0:T(8,128)S(1)}, f32[12,32]{1,0:T(8,128)}, u32[]{:S(2)}) copy-start(f32[12,32]{1,0:T(8,128)} %param.23) | copy-start | bytes 4612
  1031.4 57.7 %copy-start.29 = (f32[12,32]{1,0:T(8,128)S(1)}, f32[12,32]{1,0:T(8,128)}, u32[]{:S(2)}) copy-start(f32[12,32]{1,0:T(8,128)} %param.27) | copy-start | bytes 4612
  1031.4 57.7 %copy-start.30 = (f32[12,32]{1,0:T(8,128)S(1)}, f32[12,32]{1,0:T(8,128)}, u32[]{:S(2)}) copy-start(f32[12,32]{1,0:T(8,128)} %param.25) | copy-start | bytes 4612
  (20 other events, 46.4 us)
Sparse Core Ops, SparseCore 0:
  19.3 57.0 all-gather.3
  255.7 115.9 reduce-scatter.7
  448.7 343.1 reduce-scatter.9
  794.9 19.4 reduce-scatter.13
  817.8 207.3 reduce-scatter.11
  1028.4 59.8 reduce-scatter.15
  1090.4 27.5 all-gather.5
where the time goes:
time: 1130 us
  waiting for transfers between devices  780 us (69%)
  matrix products  151 us (13%)
  local copies, waits for them, and re-layouts  92.7 us (8%)
  other arithmetic  83.1 us (7%)
  between operations  14.9 us (1%)
    reduce_scatter x1, waiting for transfers between devices, shards(): lax.psum_scatter(regroup(grad_matrix, 0, replicas, shard_count), 'shard',...  335 us
    reduce_scatter x1, waiting for transfers between devices, shards(): lax.psum_scatter(part_matrix, ('dp', 'ctx'), scatter_dimension=0, tiled=T...  209 us
    reduce_scatter x1, waiting for transfers between devices, shards(): lax.psum_scatter(key_terms, ('ctx', 'shard'), scatter_dimension=0, tiled=...  88.6 us
    all_gather x1, waiting for transfers between devices, shards(): gathered = lax.all_gather(kv_local, ('ctx', 'shard'), axis=0, tiled=True)  55.4 us
    unnamed x8, waiting for transfers between devices  47.2 us
    transpose x2, local copies, waits for them, and re-layouts, regroup(): return jnp.swapaxes(split, dim, dim + 1).reshape(shape)  34.3 us
    concatenate x1, other arithmetic, shards(): jnp.concatenate([grad_qkv_weights, grad_proj, grad_up_w, grad_down_w], ax...  33.2 us
    dot_general x4, matrix products, weighted_sum(): jnp.einsum('hqk,khd->qhd', probs, value_heads, preferred_element_type=jnp...  22.6 us
  transfers between devices with their start and end apart: 7, of which 7 were waited for; matrix products, arithmetic and copies ran while one was open for 5% of the time, Pallas kernels for 0%

commit v1 on v0

--- a/solution.py
+++ b/solution.py
@@ -1,8 +1,11 @@
+import functools
 import math
 
 import jax
 import jax.numpy as jnp
 from jax import lax
+from jax.experimental import pallas as pl
+from jax.experimental.pallas import tpu as pltpu
 from jax.sharding import PartitionSpec as P
 
 HEADS = 16
@@ -72,7 +75,7 @@
     return (moment, variance, master - RATE * (direction + decay_rate * master))
 
 
-def shards(
+def general_shards(
     tokens,
     cotangent,
     picture_starts,
@@ -308,6 +311,471 @@
     )
 
 
+BLK=256
+f32 = jnp.float32
+bf16 = jnp.bfloat16
+NT=(((1,),(1,)),((),()))
+
+def split3(x):
+    hi=x.astype(bf16).astype(f32)
+    rest=x-hi
+    mid=rest.astype(bf16).astype(f32)
+    low=(rest-mid).astype(bf16).astype(f32)
+    return hi,mid,low
+
+def positions(index, starts_ref, count):
+    pos=index
+    for b in range(count):
+        pos=pos-jnp.clip(index-starts_ref[0,b],0,PIC-1)
+    return pos.astype(f32)
+
+def limits(index, starts_ref, count):
+    lim=index+1
+    for b in range(count):
+        s=starts_ref[0,b]
+        lim=jnp.where((index>=s)&(index<s+PIC), s+PIC, lim)
+    return lim
+
+def head_lanes(shape,h,width):
+    lane=lax.broadcasted_iota(jnp.int32,shape,1)
+    inside=(lane<width) if h==0 else (lane>=width)
+    extra=lane-width if h==0 else lane
+    return inside,extra
+
+def pick(extra,values,rest=0.0):
+    out=jnp.full(extra.shape,rest,f32)
+    for e,v in enumerate(values):
+        out=jnp.where(extra==e,v,out)
+    return out
+
+def fwd_kernel(width, tile, count, rank_ref, starts_ref, slopes_ref, qkv_ref, att_ref, o_ref, lse_ref,
+               qa, ka, va, m_ref, acc_ref):
+    seq,lanes=att_ref.shape
+    rank=rank_ref[0]
+    factor=width**-0.5
+    def prologue(t,_):
+        src=pl.ds(pl.multiple_of((t^rank)*BLK,BLK),BLK)
+        dst=pl.ds(pl.multiple_of(t*BLK,BLK),BLK)
+        q=qkv_ref[src,0:lanes].astype(f32)*factor
+        k=qkv_ref[src,lanes:2*lanes].astype(f32)
+        v=qkv_ref[src,2*lanes:3*lanes].astype(f32)
+        index=lax.broadcasted_iota(jnp.int32,(BLK,lanes),0)+t*BLK
+        pos=positions(index,starts_ref,count)
+        for h in range(2):
+            inside,extra=head_lanes((BLK,lanes),h,width)
+            hi,mid,low=split3(pos*slopes_ref[h])
+            qa[h,dst,:]=jnp.where(inside,q,pick(extra,(1.0,1.0,1.0))).astype(bf16)
+            ka[h,dst,:]=jnp.where(inside,k,pick(extra,(hi,mid,low))).astype(bf16)
+            va[h,dst,:]=jnp.where(inside,v,pick(extra,(1.0,))).astype(bf16)
+        return 0
+    lax.fori_loop(0,seq//BLK,prologue,0)
+
+    def update(h,rows,q,key_rows,mask_fn,local):
+        k=ka[h,key_rows,:]
+        v=va[h,key_rows,:]
+        s=lax.dot_general(q,k,NT,preferred_element_type=f32)
+        if mask_fn is not None:
+            s=jnp.where(mask_fn(s.shape),s,NEGATIVE)
+        old=m_ref[h,local,:]
+        best=jnp.max(s,axis=1,keepdims=True)
+        new=jnp.maximum(old,jnp.broadcast_to(best,old.shape))
+        m_ref[h,local,:]=new
+        p=jnp.exp(s-new[:,0:1]).astype(bf16)
+        pv=jnp.dot(p,v,preferred_element_type=f32)
+        acc_ref[h,local,:]=acc_ref[h,local,:]*jnp.exp(old-new)+pv
+
+    for i in range(seq//tile):
+        base=i*tile
+        m_ref[...]=jnp.full(m_ref.shape,NEGATIVE,f32)
+        acc_ref[...]=jnp.zeros(acc_ref.shape,f32)
+        def full(j,_):
+            for h in range(2):
+                update(h,None,qa[h,base:base+tile,:],pl.ds(pl.multiple_of(j*tile,tile),tile),None,slice(0,tile))
+            return 0
+        if i>0:
+            lax.fori_loop(0,i,full,0)
+        def mask(first_row,first_col,shape):
+            rows=lax.broadcasted_iota(jnp.int32,(shape[0],1),0)+first_row
+            lim=limits(rows,starts_ref,count)
+            cols=lax.broadcasted_iota(jnp.int32,shape,1)+first_col
+            return cols<lim
+        for h in range(2):
+            update(h,None,qa[h,base:base+tile,:],slice(base,base+tile),functools.partial(mask,base,base),slice(0,tile))
+        if base+tile<seq:
+            for h in range(2):
+                update(h,None,qa[h,base+tile-PIC:base+tile,:],slice(base+tile,base+tile+PIC),functools.partial(mask,base+tile-PIC,base+tile),slice(tile-PIC,tile))
+        res=[];lses=[]
+        for h in range(2):
+            acc=acc_ref[h]
+            col=width if h==0 else 0
+            total=acc[:,col:col+1]
+            res.append(acc/total)
+            lses.append(m_ref[h]+jnp.log(total))
+        inside,_=head_lanes((tile,lanes),0,width)
+        out=jnp.where(inside,res[0],res[1])
+        o_ref[base:base+tile,:]=out
+        lse_ref[base:base+tile,:]=jnp.where(inside,lses[0],lses[1])
+        att_ref[base:base+tile,:]=out.astype(bf16)
+
+def attention_forward(qkv, rank, starts, slopes, tile=512):
+    seq=qkv.shape[0]; lanes=qkv.shape[1]//3; width=lanes//2
+    count=starts.shape[1]
+    sm=pl.BlockSpec(memory_space=pltpu.SMEM)
+    vm=pl.BlockSpec(memory_space=pltpu.VMEM)
+    return pl.pallas_call(functools.partial(fwd_kernel,width,tile,count),
+        out_shape=(jax.ShapeDtypeStruct((seq,lanes),bf16),jax.ShapeDtypeStruct((seq,lanes),f32),jax.ShapeDtypeStruct((seq,lanes),f32)),
+        in_specs=[sm,sm,sm,vm], out_specs=(vm,vm,vm),
+        scratch_shapes=[pltpu.VMEM((2,seq,lanes),bf16)]*3+[pltpu.VMEM((2,tile,lanes),f32)]*2,
+        compiler_params=pltpu.CompilerParams(vmem_limit_bytes=40*2**20),
+        name="attention_forward")(rank,starts,slopes,qkv)
+
+def bwd_kernel(width, tile, count, rank_ref, starts_ref, slopes_ref, qkv_ref, do_ref, o_ref, lse_ref, abs_ref, rel_ref,
+               qa, ka, va, da, kt, dq_ref, dk_ref, dv_ref):
+    seq,lanes=do_ref.shape
+    rank=rank_ref[0]
+    factor=width**-0.5
+    def prologue(t,_):
+        src=pl.ds(pl.multiple_of((t^rank)*BLK,BLK),BLK)
+        dst=pl.ds(pl.multiple_of(t*BLK,BLK),BLK)
+        q=qkv_ref[src,0:lanes].astype(f32)*factor
+        k=qkv_ref[src,lanes:2*lanes].astype(f32)
+        v=qkv_ref[src,2*lanes:3*lanes].astype(f32)
+        kt[:,dst]=k.T.astype(bf16)
+        g=do_ref[dst,:].astype(f32)
+        prod=g*o_ref[dst,:]
+        index=lax.broadcasted_iota(jnp.int32,(BLK,lanes),0)+t*BLK
+        pos=positions(index,starts_ref,count)
+        lse=lse_ref[dst,:]
+        for h in range(2):
+            inside,extra=head_lanes((BLK,lanes),h,width)
+            hi,mid,low=split3(pos*slopes_ref[h])
+            delta=jnp.sum(jnp.where(inside,prod,0.0),axis=1,keepdims=True)
+            delta=jnp.broadcast_to(delta,(BLK,lanes))
+            lse_h=jnp.broadcast_to(lse[:,0:1] if h==0 else lse[:,width:width+1],(BLK,lanes))
+            lhi,lmid,llow=split3(-lse_h)
+            dhi,dmid,dlow=split3(-delta)
+            qa[h,dst,:]=jnp.where(inside,q,pick(extra,(1.0,1.0,1.0,lhi,lmid,llow))).astype(bf16)
+            ka[h,dst,:]=jnp.where(inside,k,pick(extra,(hi,mid,low,1.0,1.0,1.0))).astype(bf16)
+            va[h,dst,:]=jnp.where(inside,v,pick(extra,(1.0,1.0,1.0))).astype(bf16)
+            da[h,dst,:]=jnp.where(inside,g,pick(extra,(dhi,dmid,dlow))).astype(bf16)
+        return 0
+    lax.fori_loop(0,seq//BLK,prologue,0)
+    dq_ref[...]=jnp.zeros(dq_ref.shape,f32)
+
+    def pair(h,key_rows,query_rows,mask_fn,dkv_rows):
+        st=lax.dot_general(ka[h,key_rows,:],qa[h,query_rows,:],NT,preferred_element_type=f32)
+        pt=jnp.exp(st)
+        if mask_fn is not None:
+            pt=jnp.where(mask_fn(st.shape),pt,0.0)
+        dpt=lax.dot_general(va[h,key_rows,:],da[h,query_rows,:],NT,preferred_element_type=f32)
+        dst=(pt*dpt).astype(bf16)
+        dv_ref[h,dkv_rows,:]+=jnp.dot(pt.astype(bf16),da[h,query_rows,:],preferred_element_type=f32)
+        dk_ref[h,dkv_rows,:]+=jnp.dot(dst,qa[h,query_rows,:],preferred_element_type=f32)
+        rows=slice(h*width,(h+1)*width)
+        dq_ref[rows,query_rows]+=jnp.dot(kt[rows,key_rows],dst,preferred_element_type=f32)
+
+    for j in range(seq//tile):
+        base=j*tile
+        dk_ref[...]=jnp.zeros(dk_ref.shape,f32)
+        dv_ref[...]=jnp.zeros(dv_ref.shape,f32)
+        def mask(first_key,first_query,shape):
+            cols=lax.broadcasted_iota(jnp.int32,(1,shape[1]),1)+first_query
+            lim=limits(cols,starts_ref,count)
+            rows=lax.broadcasted_iota(jnp.int32,shape,0)+first_key
+            return rows<lim
+        if base>0:
+            for h in range(2):
+                pair(h,slice(base,base+PIC),slice(base-PIC,base),functools.partial(mask,base,base-PIC),slice(0,PIC))
+        for h in range(2):
+            pair(h,slice(base,base+tile),slice(base,base+tile),functools.partial(mask,base,base),slice(0,tile))
+        def full(i,_):
+            for h in range(2):
+                pair(h,slice(base,base+tile),pl.ds(pl.multiple_of(i*tile,tile),tile),None,slice(0,tile))
+            return 0
+        if base+tile<seq:
+            lax.fori_loop(j+1,seq//tile,full,0)
+        inside,_=head_lanes((BLK,lanes),0,width)
+        for t in range(tile//BLK):
+            part=slice(t*BLK,(t+1)*BLK)
+            dst=pl.ds(pl.multiple_of(((j*(tile//BLK)+t)^rank)*BLK,BLK),BLK)
+            dk=jnp.where(inside,dk_ref[0,part,:],dk_ref[1,part,:]).astype(bf16)
+            dv=jnp.where(inside,dv_ref[0,part,:],dv_ref[1,part,:]).astype(bf16)
+            same=slice(base+t*BLK,base+(t+1)*BLK)
+            for ref,rows in ((abs_ref,same),(rel_ref,dst)):
+                ref[rows,lanes:2*lanes]=dk
+                ref[rows,2*lanes:3*lanes]=dv
+    for t in range(seq//BLK):
+        dst=pl.ds(pl.multiple_of((t^rank)*BLK,BLK),BLK)
+        dq=(dq_ref[:,t*BLK:(t+1)*BLK].T*factor).astype(bf16)
+        abs_ref[t*BLK:(t+1)*BLK,0:lanes]=dq
+        rel_ref[dst,0:lanes]=dq
+
+def attention_backward(qkv, do, o, lse, rank, starts, slopes, tile=512):
+    seq=qkv.shape[0]; lanes=qkv.shape[1]//3; width=lanes//2
+    count=starts.shape[1]
+    sm=pl.BlockSpec(memory_space=pltpu.SMEM)
+    vm=pl.BlockSpec(memory_space=pltpu.VMEM)
+    return pl.pallas_call(functools.partial(bwd_kernel,width,tile,count),
+        out_shape=(jax.ShapeDtypeStruct((seq,3*lanes),bf16),)*2,
+        in_specs=[sm,sm,sm,vm,vm,vm,vm], out_specs=(vm,vm),
+        scratch_shapes=[pltpu.VMEM((2,seq,lanes),bf16)]*4+[pltpu.VMEM((lanes,seq),bf16),pltpu.VMEM((lanes,seq),f32)]+[pltpu.VMEM((2,tile,lanes),f32)]*2,
+        compiler_params=pltpu.CompilerParams(vmem_limit_bytes=40*2**20),
+        name="attention_backward")(rank,starts,slopes,qkv,do,o,lse)
+
+
+def fits_sequence_plan(mesh):
+    return mesh.shape["dp"] == 4 and mesh.shape["ctx"] == 2 and mesh.shape["shard"] == 4
+
+
+def swap(array, axis, bit):
+    count = lax.axis_size(axis)
+    return lax.ppermute(array, axis, [(i, i ^ bit) for i in range(count)])
+
+
+def gather_sequence(block):
+    over_ctx = swap(block, "ctx", 1)
+    over_y = swap(block, "shard", 2)
+    over_core = swap(block, "shard", 1)
+    core = lax.axis_index("shard") % 2
+    relay = jnp.where(core == 0, over_ctx, over_y)
+    opposite = lax.ppermute(
+        relay, ("ctx", "shard"), [(i, i ^ (2 if i % 2 == 0 else 4)) for i in range(8)]
+    )
+    ctx_core = swap(over_ctx, "shard", 1)
+    y_core = swap(over_y, "shard", 1)
+    opposite_core = swap(opposite, "shard", 1)
+    return jnp.concatenate(
+        [block, over_core, over_y, y_core, over_ctx, ctx_core, opposite, opposite_core], axis=0
+    )
+
+
+def exchange(array):
+    return lax.all_to_all(array, ("ctx", "shard"), 0, 0, tiled=True)
+
+
+def dot_tn(left, right):
+    return lax.dot_general(left, right, (((0,), (0,)), ((), ())), preferred_element_type=f32)
+
+
+def dot_nt(left, right):
+    return lax.dot_general(left, right, (((1,), (1,)), ((), ())), preferred_element_type=f32)
+
+
+def dot_nn(left, right):
+    return jnp.dot(left, right, preferred_element_type=f32)
+
+
+def sum_over_dp(lhs, rhs, extra=None):
+    quarter = lhs.shape[1] // 4
+    send = dot_tn(lhs[:, : 2 * quarter], rhs).astype(bf16)
+    got = lax.ppermute(send, "dp", [(i, i ^ 1) for i in range(4)])
+    relay = (dot_tn(lhs[:, 2 * quarter : 3 * quarter], rhs) + got[quarter:].astype(f32)).astype(bf16)
+    far = lax.ppermute(relay, "dp", [(i, 3 - i) for i in range(4)])
+    return dot_tn(lhs[:, 3 * quarter :], rhs) + got[:quarter].astype(f32) + far.astype(f32)
+
+
+def sequence_shards(
+    tokens,
+    cotangent,
+    picture_starts,
+    matrices,
+    vectors,
+    master_matrices,
+    master_vectors,
+    first_matrices,
+    first_vectors,
+    second_matrices,
+    second_vectors,
+):
+    row_count, width = tokens.shape
+    ff_width = (matrices.shape[1] - 4 * width) // 2
+    head_width = width // HEADS
+    group = 8
+    rank = lax.axis_index("ctx") * 4 + lax.axis_index("shard")
+    depth = lax.axis_index("dp")
+    lanes = width // group
+    units = ff_width // group
+    heads_here = HEADS // group
+    head = rank * heads_here + jnp.arange(heads_here)
+    slopes = jnp.exp2(-8.0 * (head.astype(f32) + 1.0) / HEADS)
+    rank_array = rank.astype(jnp.int32).reshape(1)
+    quarter = width // 4
+    near = depth ^ 1
+    order = [near, 3 - near, 3 - depth, depth]
+
+    def reorder(array, dim):
+        return jnp.concatenate(
+            [lax.dynamic_slice_in_dim(array, block * quarter, quarter, dim) for block in order],
+            axis=dim,
+        )
+
+    def own(first, size):
+        return reorder(lax.dynamic_slice_in_dim(matrices, first + rank * size, size, 1), 0)
+
+    w_qkv = matrices[:, : 3 * width]
+    w_proj = matrices[:, 3 * width : 4 * width]
+    w_up = matrices[:, 4 * width : 4 * width + ff_width]
+    w_down = matrices[:, 4 * width + ff_width :]
+    inputs = tokens.astype(f32)
+    vector_rows = vectors.astype(f32)
+    up_bias = vector_rows[8:].reshape(ff_width)
+
+    with jax.named_scope("norm_one"):
+        normed, inverse_std = layer_norm(inputs)
+        hidden = (normed * vector_rows[0] + vector_rows[1]).astype(bf16)
+    with jax.named_scope("gather_hidden"):
+        hidden_all = gather_sequence(reorder(hidden, 1))
+    with jax.named_scope("project"):
+        w_heads = jnp.concatenate([own(0, lanes), own(width, lanes), own(2 * width, lanes)], axis=1)
+        bias = jnp.concatenate(
+            [
+                lax.dynamic_slice_in_dim(vector_rows[2], rank * lanes, lanes, 0),
+                jnp.zeros((lanes,), f32),
+                lax.dynamic_slice_in_dim(vector_rows[3], rank * lanes, lanes, 0),
+            ]
+        )
+        qkv = (dot_nn(hidden_all, w_heads) + bias).astype(bf16)
+    attended_heads, attended_wide, log_total = attention_forward(
+        qkv, rank_array, picture_starts, slopes
+    )
+    with jax.named_scope("attended_exchange"):
+        attended = (
+            exchange(attended_heads.reshape(group, row_count, lanes))
+            .transpose(1, 0, 2)
+            .reshape(row_count, width)
+        )
+    with jax.named_scope("gather_cotangent"):
+        cotangent_all = gather_sequence(reorder(cotangent, 1))
+    with jax.named_scope("feed_forward"):
+        middle = inputs + dot_nn(attended, w_proj) + vector_rows[4]
+        normed_two, inverse_two = layer_norm(middle)
+        hidden_two = (normed_two * vector_rows[5] + vector_rows[6]).astype(bf16)
+        pre_act = dot_nn(hidden_two, w_up) + up_bias
+        grad_act = dot_nn(cotangent, w_down)
+        act, pull = jax.vjp(activate, pre_act)
+        act_low = act.astype(bf16)
+        grad_pre = pull(grad_act)[0].astype(bf16)
+        grad_two = dot_nt(grad_pre, w_up)
+        upstream = cotangent.astype(f32)
+        grad_mid = upstream + norm_backward(grad_two, vector_rows[5], normed_two, inverse_two)
+        grad_mid_low = grad_mid.astype(bf16)
+        grad_attended = dot_nt(grad_mid_low, w_proj).astype(bf16)
+    with jax.named_scope("grad_attended_exchange"):
+        grad_heads = exchange(
+            grad_attended.reshape(row_count, group, lanes).transpose(1, 0, 2)
+        ).reshape(group * row_count, lanes)
+    with jax.named_scope("layer_output"):
+        layer_output = (middle + dot_nt(act_low, w_down) + vector_rows[7]).astype(bf16)
+    with jax.named_scope("gather_hidden_two"):
+        hidden_two_all = gather_sequence(reorder(hidden_two, 1))
+    with jax.named_scope("own_units"):
+        own_up = own(4 * width, units)
+        own_down = own(4 * width + ff_width, units)
+        own_pre = dot_nn(hidden_two_all, own_up) + lax.dynamic_slice_in_dim(
+            up_bias, rank * units, units, 0
+        )
+        own_grad_act = dot_nn(cotangent_all, own_down)
+        own_act, own_pull = jax.vjp(activate, own_pre)
+        own_act_low = own_act.astype(bf16)
+        own_grad_pre = own_pull(own_grad_act)[0].astype(bf16)
+    with jax.named_scope("grad_down"):
+        sum_down = sum_over_dp(cotangent_all, own_act_low)
+    with jax.named_scope("grad_up"):
+        sum_up = sum_over_dp(hidden_two_all, own_grad_pre)
+    with jax.named_scope("grad_proj"):
+        grad_proj = dot_tn(attended, grad_mid_low).astype(bf16)
+        grad_proj = (
+            grad_proj.reshape(4, group, 32, width).transpose(1, 0, 2, 3).reshape(group, 128, width)
+        )
+        part_proj = lax.psum_scatter(
+            grad_proj.reshape(width, width), ("ctx", "shard"), scatter_dimension=0, tiled=True
+        )
+        part_proj = lax.psum_scatter(part_proj, "dp", scatter_dimension=0, tiled=True).astype(f32)
+    grad_abs, grad_rel = attention_backward(
+        qkv, grad_heads, attended_wide, log_total, rank_array, picture_starts, slopes
+    )
+    with jax.named_scope("grad_qkv_exchange"):
+        grad_qkv = (
+            exchange(grad_abs.reshape(group, row_count, 3 * lanes))
+            .reshape(group, row_count, 3, lanes)
+            .transpose(1, 2, 0, 3)
+            .reshape(row_count, 3 * width)
+        )
+    with jax.named_scope("grad_qkv_weights"):
+        sum_qkv = sum_over_dp(hidden_all, grad_rel)
+        own_bias_grad = jnp.sum(grad_rel.astype(f32), axis=0)
+    with jax.named_scope("grad_hidden"):
+        grad_hidden = dot_nt(grad_qkv, w_qkv)
+        token_grads = grad_mid + norm_backward(grad_hidden, vector_rows[0], normed, inverse_std)
+    with jax.named_scope("grad_vectors"):
+
+        def spread(values, total):
+            return lax.dynamic_update_slice_in_dim(
+                jnp.zeros((total,), f32), values, rank * values.shape[0], 0
+            )
+
+        grad_vectors = jnp.concatenate(
+            [
+                jnp.stack(
+                    [
+                        jnp.sum(grad_hidden * normed, axis=0),
+                        jnp.sum(grad_hidden, axis=0),
+                        spread(own_bias_grad[:lanes], width),
+                        spread(own_bias_grad[2 * lanes :], width),
+                        jnp.sum(grad_mid, axis=0),
+                        jnp.sum(grad_two * normed_two, axis=0),
+                        jnp.sum(grad_two, axis=0),
+                        jnp.sum(upstream, axis=0),
+                    ]
+                ),
+                spread(jnp.sum(own_grad_pre.astype(f32), axis=0), ff_width).reshape(-1, width),
+            ],
+            axis=0,
+        )
+        summed = lax.psum(grad_vectors, ("dp", "ctx", "shard"))
+        part_vec = lax.dynamic_slice_in_dim(summed, (depth * group + rank) * 32, 32, 1)
+    with jax.named_scope("rows_exchange"):
+
+        def to_rows(array, parts):
+            columns = array.shape[1]
+            got = exchange(array.astype(bf16).reshape(group, 32, columns))
+            got = got.reshape(group, 32, parts, columns // parts).transpose(1, 2, 0, 3)
+            return got.reshape(32, group * columns).astype(f32)
+
+        part_matrix = jnp.concatenate(
+            [to_rows(sum_qkv, 3), part_proj, to_rows(sum_up, 1), to_rows(sum_down, 1)], axis=1
+        )
+    root = (row_count * lax.axis_size("dp") * group) ** (-0.5)
+    correction = 1.0 - BETA**STEP
+    with jax.named_scope("update"):
+        moment_w, variance_w, updated_w = adam_update(
+            master_matrices,
+            first_matrices,
+            second_matrices,
+            part_matrix * root,
+            correction,
+            DECAY_RATE,
+        )
+        moment_v, variance_v, updated_v = adam_update(
+            master_vectors, first_vectors, second_vectors, part_vec * root, correction, 0.0
+        )
+    with jax.named_scope("copies"):
+        copied_w = lax.all_gather(updated_w.astype(bf16), "shard", axis=0, tiled=True)
+        copied_v = lax.all_gather(updated_v.astype(bf16), "shard", axis=1, tiled=True)
+    return (
+        layer_output,
+        token_grads,
+        moment_w,
+        moment_v,
+        variance_w,
+        variance_v,
+        updated_w,
+        updated_v,
+        copied_w,
+        copied_v,
+    )
+
+
 def solution(mesh):
     in_specs = (
         P(("dp", "ctx", "shard"), None),
@@ -334,4 +802,5 @@
         P(("dp", "ctx"), None),
         P(None, ("dp", "ctx")),
     )
-    return jax.shard_map(shards, mesh=mesh, in_specs=in_specs, out_specs=out_specs, check_vma=False)
+    body = sequence_shards if fits_sequence_plan(mesh) else general_shards
+    return jax.shard_map(body, mesh=mesh, in_specs=in_specs, out_specs=out_specs, check_vma=False)

time: 1130 us -> 375 us (0.33)
  waiting for transfers between devices: 780 us -> 62.1 us
  matrix products: 151 us -> 75.4 us
  other arithmetic: 83.1 us -> 22.9 us
  starting transfers between devices: 0.85 us -> 51.4 us
  Pallas kernels: 0 us -> 45.1 us
  local copies, waits for them, and re-layouts: 92.7 us -> 50.5 us
  blocking collectives: 5.17 us -> 45.5 us
    reduce_scatter x4 -> x2, waiting for transfers between devices: 655 us -> 1.38 us  [the longest x1 1.38 us: sequence_shards(): lax.psum_scatter(part_proj, 'dp', scatter_dimension=0, tiled=True)]
    all_gather x2 -> x1, waiting for transfers between devices: 77.8 us -> 0.01 us  [sequence_shards(): lax.all_gather(updated_w.astype(bf16), 'shard', axis=0, tiled=True)]
    dot_general x40 -> x19, matrix products: 151 us -> 75.4 us  [the longest x4 29.3 us: dot_nt(): lax.dot_general(left, right, (((1,), (1,)), ((), ())), preferred_element_...]
    unnamed x8 -> x3, waiting for transfers between devices: 47.2 us -> 0.05 us
    pallas_call x0 -> x2, Pallas kernels: none -> 45.1 us  [the longest x1 22.7 us: attention_forward(): pl.pallas_call(functools.partial(fwd_kernel, width, tile, count), out_sha...]
    psum x0 -> x1, blocking collectives: none -> 40 us  [sequence_shards(): summed = lax.psum(grad_vectors, ('dp', 'ctx', 'shard'))]
    ppermute x0 -> x27, waiting for transfers between devices: none -> 32 us  [the longest x18 10.9 us: swap(): return lax.ppermute(array, axis, [(i, i ^ bit) for i in range(count)])]
    transpose x2, local copies, waits for them, and re-layouts: 34.3 us -> 3.16 us  [the longest x1 1.62 us: sequence_shards(): grad_proj.reshape(4, group, 32, width).transpose(1, 0, 2, 3)]
  transfers between devices with their start and end apart: 7 -> 36, of which waited for: 7 -> 11; matrix products, arithmetic and copies ran while one was open for 5% -> 34% of each run, Pallas kernels for 0% -> 12%
where the time goes in v1:
time: 375 us; the launch traced here: 368 us
  matrix products  75.4 us (20%)
  waiting for transfers between devices  62.1 us (17%)
  starting transfers between devices  51.4 us (14%)
  local copies, waits for them, and re-layouts  50.5 us (13%)
  blocking collectives  45.5 us (12%)
  Pallas kernels  45.1 us (12%)
  other arithmetic  22.9 us (6%)
  between operations  15.2 us (4%)
    psum x1, blocking collectives, sequence_shards(): summed = lax.psum(grad_vectors, ('dp', 'ctx', 'shard'))  40 us
    unnamed x112, local copies, waits for them, and re-layouts  29.5 us
    dot_general x4, matrix products, dot_nt(): lax.dot_general(left, right, (((1,), (1,)), ((), ())), preferred_element_...  29.3 us
    all_to_all x6, starting transfers between devices, exchange(): return lax.all_to_all(array, ('ctx', 'shard'), 0, 0, tiled=True)  28.9 us
    all_to_all x6, waiting for transfers between devices, exchange(): return lax.all_to_all(array, ('ctx', 'shard'), 0, 0, tiled=True)  28.7 us
    dot_general x5, matrix products, dot_nn(): return jnp.dot(left, right, preferred_element_type=f32)  24.2 us
    pallas_call x1, Pallas kernels, attention_forward(): pl.pallas_call(functools.partial(fwd_kernel, width, tile, count), out_sha...  22.7 us
    pallas_call x1, Pallas kernels, attention_backward(): pl.pallas_call(functools.partial(bwd_kernel, width, tile, count), out_sha...  22.4 us
  transfers between devices with their start and end apart: 36, of which 11 were waited for; matrix products, arithmetic and copies ran while one was open for 34% of the time, Pallas kernels for 12%

profile of v1, /device:TPU:0, one launch (start us, length us, event | category | flops | bytes accessed | tf_op | source)
XLA Modules:
  0.0 368.1 jit_solution(14607056748543030485)
XLA Ops:
  21.7 8.9 %collective-permute-done.1 = bf16[256,1024]{1,0:T(8,128)(2,1)S(1)} collective-permute-done((bf16[256,1024]{1,0:T(8,128)(2,1)S(1)}, bf16[256,1024]{1,0:T(8,128)(2,1)S(1)}, u32[]{:S(2)}, u32[]{:S(2)}) %collective-permute-start.1) | collective-permute-done | bytes 524320 | tf_op jit(solution)/shard_map/gather_hidden/ppermute | solution.py:532
  37.5 9.8 %collective-permute-done.5 = bf16[256,1024]{1,0:T(8,128)(2,1)S(1)} collective-permute-done((bf16[256,1024]{1,0:T(8,128)(2,1)S(1)}, bf16[256,1024]{1,0:T(8,128)(2,1)S(1)}, u32[]{:S(2)}, u32[]{:S(2)}) %collective-permute-start.5) | collective-permute-done | bytes 524320 | tf_op jit(solution)/shard_map/gather_hidden/ppermute | solution.py:541
  54.3 22.7 %attention_forward.1 = (bf16[2048,128]{1,0:T(8,128)(2,1)S(1)}, f32[2048,128]{1,0:T(8,128)S(1)}, f32[2048,128]{1,0:T(8,128)S(1)}) custom-call(s32[1]{0:T(128)} %bitcast.rank_ref, s32[1,7]{1,0:T(1,128)S(1)} %copy-done.8, f32[2]{0:T(128)S(1)} %multiply_exponential_fusion.slopes_ref, bf16[2048,384]{1,0:T(8,128)(2,1)S(1)} %add_convert_fusion.qkv_ref), custom_call_target="tpu_custom_call" | custom-call | tf_op jit(solution)/shard_map/attention_forward/pallas_call | solution.py:425
  84.3 4.9 %fusion.174 = (bf16[256,512]{1,0:T(8,128)(2,1)}, bf16[256,512]{1,0:T(8,128)(2,1)}, bf16[256,512]{1,0:T(8,128)(2,1)}, bf16[256,512]{1,0:T(8,128)(2,1)}, bf16[256,...) fusion(bf16[1024,12288]{1,0:T(8,128)(2,1)} %param.14, ...), kind=kLoop, calls=%fused_computation.240 | loop fusion | bytes 4194328 | tf_op jit(solution)/shard_map/own_units/dynamic_slice | solution.py:608
  95.8 7.7 %fusion.10 = f32[256,4096]{1,0:T(8,128)} fusion(bf16[256,1024]{1,0:T(8,128)(2,1)S(1)} %add_convert_fusion.1, bf16[1024,12288]{1,0:T(8,128)(2,1)} %param.14, f32[4096]{0:T(1024)S(1)} %bitcast.122), kind=kOutput, calls=%fused_computation.14 | convolution fusion | flops 2148532224 | bytes 13123584 | tf_op jit(solution)/shard_map/feed_forward/dot_general | solution.py:565
  106.1 12.9 %multiply_reduce_fusion = (f32[1024]{0:T(1024)}, f32[256]{0:T(256)S(1)}, f32[256]{0:T(256)S(1)}, f32[1024]{0:T(1024)}, f32[256,1024]{1,0:T(8,128)}) fusion(f32[256,1024]{1,0:T(8,128)S(1)} %get-tuple-element.92, f32[256]{0:T(256)S(1)} %add_rsqrt_fusion, f32[256]{0:T(256)S(1)} %broadcast_multiply_fusion.4, f32[1024]{0:T(1024)S(1)} %bitcast.118, ...), kind=kOutput, calls=%fused_computation.126 | convolution fusion | flops 4318296064 | bytes 23609344 | tf_op jit(solution)/shard_map/feed_forward/dot_general | solution.py:561
  124.9 4.2 %all-to-all-start.1 = ((bf16[8,256,128]{2,1,0:T(8,128)(2,1)}), bf16[8,256,128]{2,1,0:T(8,128)(2,1)S(1)}, u32[]{:S(2)}, u32[]{:S(2)}) async-start(bf16[8,256,128]{2,1,0:T(8,128)(2,1)} %bitcast.96), calls=%async_computation.1 | async-start | bytes 1048576 | tf_op jit(solution)/shard_map/grad_attended_exchange/all_to_all | solution.py:553
  143.2 22.4 %attention_backward.1 = (bf16[2048,384]{1,0:T(8,128)(2,1)S(1)}, bf16[2048,384]{1,0:T(8,128)(2,1)S(1)}) custom-call(s32[1]{0:T(128)} %bitcast.rank_ref, s32[1,7]{1,0:T(1,128)S(1)} %copy-done.8, f32[2]{0:T(128)S(1)} %multiply_exponential_fusion.slopes_ref, bf16[2048,384]{1,0:T(8,128)(2,1)S(1)} %add_convert_fusion.qkv_ref, bf16[2048,128]{1,0:T(8,128)(2,1)S(1)} %bitcast.99, ...), custom_call_target="tpu_custom_call" | custom-call | tf_op jit(solution)/shard_map/attention_backward/pallas_call | solution.py:518
  185.2 3.7 collective-permute-start.8
  194.2 5.8 %multiply_convert_fusion = (bf16[2048,512]{1,0:T(8,128)(2,1)S(1)}, f32[2048,512]{1,0:T(8,128)S(1)}) fusion(f32[512]{0:T(512)S(1)} %copy-done.39, bf16[2048,1024]{1,0:T(8,128)(2,1)} %constant_dynamic-update-slice_fusion.8, bf16[256,512]{1,0:T(8,128)(2,1)S(1)} %copy-done.26, bf16[256,512]{1,0:T(8,128)(2,1)S(1)} %copy-done.27, ...), kind=kOutput, calls=%fused_computation.30 | convolution fusion | flops 2162163712 | bytes 11536384 | tf_op jit(solution)/shard_map/own_units/dot_general | solution.py:565
  202.4 5.5 %convert_reduce_fusion = (f32[512]{0:T(512)}, bf16[2048,512]{1,0:T(8,128)(2,1)S(1)}) fusion(f32[2048,512]{1,0:T(8,128)S(1)} %get-tuple-element.96, f32[512]{0:T(512)S(1)} %copy-done.39, bf16[2048,1024]{1,0:T(8,128)(2,1)S(1)} %copy-done.29, bf16[256,512]{1,0:T(8,128)(2,1)S(1)} %copy-done.21, bf16[256,512]{1,0:T(8,128)(2,1)S(1)} %copy-done.22, ...), kind=kOutput, calls=%fused_computation.29 | convolution fusion | flops 2175794688 | bytes 11538432 | tf_op jit(solution)/shard_map/own_units/dot_general | solution.py:565
  214.0 3.8 %all-to-all-start.3 = ((bf16[8,32,384]{2,1,0:T(8,128)(2,1)}), bf16[8,32,384]{2,1,0:T(8,128)(2,1)S(1)}, u32[]{:S(2)}, u32[]{:S(2)}) async-start(bf16[8,32,384]{2,1,0:T(8,128)(2,1)} %bitcast.18), calls=%async_computation.3 | async-start | bytes 393216 | tf_op jit(solution)/shard_map/rows_exchange/all_to_all | solution.py:553
  221.1 3.7 %collective-permute-done.23 = bf16[512,512]{1,0:T(8,128)(2,1)S(1)} collective-permute-done((bf16[512,512]{1,0:T(8,128)(2,1)S(1)}, bf16[512,512]{1,0:T(8,128)(2,1)S(1)}, u32[]{:S(2)}, u32[]{:S(2)}) %collective-permute-start.23) | collective-permute-done | bytes 524320 | tf_op jit(solution)/shard_map/grad_up/ppermute | solution.py:571
  227.3 4.6 %collective-permute-done.26 = bf16[256,512]{1,0:T(8,128)(2,1)S(1)} collective-permute-done((bf16[256,512]{1,0:T(8,128)(2,1)S(1)}, bf16[256,512]{1,0:T(8,128)(2,1)S(1)}, u32[]{:S(2)}, u32[]{:S(2)}) %collective-permute-start.26) | collective-permute-done | bytes 262176 | tf_op jit(solution)/shard_map/grad_down/ppermute | solution.py:573
  234.6 9.2 %all-to-all-start.5 = ((bf16[8,32,512]{2,1,0:T(8,128)(2,1)}), bf16[8,32,512]{2,1,0:T(8,128)(2,1)S(1)}, u32[]{:S(2)}, u32[]{:S(2)}) async-start(bf16[8,32,512]{2,1,0:T(8,128)(2,1)} %bitcast.27), calls=%async_computation.7 | async-start | bytes 524288 | tf_op jit(solution)/shard_map/rows_exchange/all_to_all | solution.py:553
  254.4 4.9 %all-to-all-done.4 = bf16[8,32,512]{2,1,0:T(8,128)(2,1)S(1)} async-done(((bf16[8,32,512]{2,1,0:T(8,128)(2,1)}), bf16[8,32,512]{2,1,0:T(8,128)(2,1)S(1)}, u32[]{:S(2)}, u32[]{:S(2)}) %all-to-all-start.4) | async-done | bytes 262176 | tf_op jit(solution)/shard_map/rows_exchange/all_to_all | solution.py:553
  261.4 5.8 %fusion.170 = (bf16[32,12288]{1,0:T(8,128)(2,1)}, f32[32,12288]{1,0:T(8,128)}, f32[32,12288]{1,0:T(8,128)}, f32[32,12288]{1,0:T(8,128)}) fusion(f32[32,12288]{1,0:T(8,128)} %param.16, bf16[32,4096]{1,0:T(8,128)(2,1)S(1)} %bitcast.107, bf16[32,4096]{1,0:T(8,128)(2,1)} %bitcast.108, bf16[32,1024]{1,0:T(8,128)(2,1)} %reduce-scatter.5.cloned.1.call-done, ...), kind=kLoop, calls=%fused_computation.238 | loop fusion | flops 9437184 | bytes 11010048 | tf_op jit(solution)/shard_map/copies/convert_element_type | solution.py:763
  268.9 4.6 %all-to-all-start.2 = ((bf16[8,256,384]{1,2,0:T(8,128)(2,1)}), bf16[8,256,384]{1,2,0:T(8,128)(2,1)}, u32[]{:S(2)}, u32[]{:S(2)}) async-start(bf16[8,256,384]{1,2,0:T(8,128)(2,1)} %copy.54), calls=%async_computation.2 | async-start | bytes 3145728 | tf_op jit(solution)/shard_map/grad_qkv_exchange/all_to_all | solution.py:553
  273.5 8.9 %fusion.65 = bf16[256,1024]{1,0:T(8,128)(2,1)} fusion(f32[256,1024]{1,0:T(8,128)} %copy-done.9, bf16[1024,12288]{1,0:T(8,128)(2,1)} %param.14, f32[256,4096]{1,0:T(8,128)} %fusion.10, f32[1024]{0:T(1024)S(1)} %bitcast.127), kind=kOutput, calls=%fused_computation.69 | convolution fusion | flops 2157707264 | bytes 14159872 | tf_op jit(solution)/shard_map/layer_output/dot_general | solution.py:561
  283.2 18.9 %all-to-all-done.2 = bf16[8,256,384]{1,2,0:T(8,128)(2,1)} async-done(((bf16[8,256,384]{1,2,0:T(8,128)(2,1)}), bf16[8,256,384]{1,2,0:T(8,128)(2,1)}, u32[]{:S(2)}, u32[]{:S(2)}) %all-to-all-start.2) | async-done | bytes 1572896 | tf_op jit(solution)/shard_map/grad_qkv_exchange/all_to_all | solution.py:553
  303.7 5.1 %fusion.104 = (f32[1024]{0:T(1024)S(1)}, f32[256]{0:T(256)S(1)}, f32[256]{0:T(256)S(1)}, f32[1024]{0:T(1024)S(1)}, f32[256,1024]{1,0:T(8,128)S(1)}) fusion(bf16[256,1024]{1,0:T(8,128)(2,1)S(1)} %copy-done.10, f32[256]{0:T(256)S(1)} %copy-done.32, f32[256]{0:T(256)S(1)} %broadcast_multiply_fusion.5, f32[1024]{0:T(1024)S(1)} %bitcast.115, ...), kind=kOutput, calls=%fused_computation.102 | convolution fusion | flops 1613231616 | bytes 9453568 | tf_op jit(solution)/shard_map/grad_hidden/dot_general | solution.py:561
  308.9 40.0 %psum.7 = f32[12,1024]{1,0:T(8,128)S(1)} all-reduce(f32[12,1024]{1,0:T(8,128)S(1)} %concatenate.63), channel_id=1, replica_groups=mesh['dp'=4,'ctx'=2,'shard'=4] {'dp','ctx','shard'}, use_global_device_ids=true, to_apply=%region_18.19 | all-reduce | flops 12288 | bytes 98304 | tf_op jit(solution)/shard_map/grad_vectors/psum | solution.py:735
  349.7 5.5 %all-gather = bf16[4,32,12]{1,2,0:T(8,128)(2,1)S(1)} all-gather(bf16[1,32,12]{1,2,0:T(8,128)(2,1)S(1)} %get-tuple-element.28), channel_id=1, replica_groups=mesh['dp'=4,'ctx'=2,'shard'=4] {'shard'}, dimensions={0}, use_global_device_ids=true | all-gather | bytes 3840 | tf_op jit(solution)/shard_map/copies/all_gather | solution.py:764
  357.2 3.8 %copy.99 = bf16[128,12288]{1,0:T(8,128)(2,1)} copy(bf16[128,12288]{1,0:T(8,128)(2,1)} %all-gather.3.cloned.1.call-done) | data formatting | bytes 6291456
  (240 shorter events, 125.6 us)
Async XLA Ops:
  15.3 15.3 %collective-permute-start.1 = (bf16[256,1024]{1,0:T(8,128)(2,1)S(1)}, bf16[256,1024]{1,0:T(8,128)(2,1)S(1)}, u32[]{:S(2)}, u32[]{:S(2)}) collective-permute-start(bf16[256,1024]{1,0:T(8,128)(2,1)S(1)} %get-tuple-element.77), channel_id=1, source_target_pairs={{0,2},{1,3},{2,0},{3,1},{4,6},{5,7},{6,4},{7,5},{8,10},{9,11},{10,... | collective-permute-start | bytes 1572872 | tf_op jit(solution)/shard_map/gather_hidden/ppermute | solution.py:532
  17.8 14.8 %collective-permute-start.3 = (bf16[256,1024]{1,0:T(8,128)(2,1)S(1)}, bf16[256,1024]{1,0:T(8,128)(2,1)S(1)}, u32[]{:S(2)}, u32[]{:S(2)}) collective-permute-start(bf16[256,1024]{1,0:T(8,128)(2,1)S(1)} %get-tuple-element.77), channel_id=1, source_target_pairs={{0,4},{4,0},{1,5},{5,1},{2,6},{6,2},{3,7},{7,3},{8,12},{12,8},{9,1... | collective-permute-start | bytes 1572872 | tf_op jit(solution)/shard_map/gather_hidden/ppermute | solution.py:532
  20.2 28.3 %collective-permute-start.17 = (bf16[256,1024]{1,0:T(8,128)(2,1)S(1)}, bf16[256,1024]{1,0:T(8,128)(2,1)}, u32[]{:S(2)}, u32[]{:S(2)}) collective-permute-start(bf16[256,1024]{1,0:T(8,128)(2,1)S(1)} %get-tuple-element.61), channel_id=1, source_target_pairs={{0,2},{1,3},{2,0},{3,1},{4,6},{5,7},{6,4},{7,5},{8,10},{9,11},{10,... | collective-permute-start | bytes 1572872 | tf_op jit(solution)/shard_map/gather_cotangent/ppermute | solution.py:532
  20.7 15.4 %collective-permute-start.16 = (bf16[256,1024]{1,0:T(8,128)(2,1)S(1)}, bf16[256,1024]{1,0:T(8,128)(2,1)S(1)}, u32[]{:S(2)}, u32[]{:S(2)}) collective-permute-start(bf16[256,1024]{1,0:T(8,128)(2,1)S(1)} %get-tuple-element.61), channel_id=1, source_target_pairs={{0,1},{1,0},{2,3},{3,2},{4,5},{5,4},{6,7},{7,6},{8,9},{9,8},{10,11... | collective-permute-start | bytes 1572872 | tf_op jit(solution)/shard_map/gather_cotangent/ppermute | solution.py:532
  20.7 27.8 %collective-permute-start.19 = (bf16[256,1024]{1,0:T(8,128)(2,1)S(1)}, bf16[256,1024]{1,0:T(8,128)(2,1)}, u32[]{:S(2)}, u32[]{:S(2)}) collective-permute-start(bf16[256,1024]{1,0:T(8,128)(2,1)S(1)} %get-tuple-element.61), channel_id=1, source_target_pairs={{0,4},{4,0},{1,5},{5,1},{2,6},{6,2},{3,7},{7,3},{8,12},{12,8},{9,1... | collective-permute-start | bytes 1572872 | tf_op jit(solution)/shard_map/gather_cotangent/ppermute | solution.py:532
  36.0 15.5 %collective-permute-start.2 = (bf16[256,1024]{1,0:T(8,128)(2,1)S(1)}, bf16[256,1024]{1,0:T(8,128)(2,1)S(1)}, u32[]{:S(2)}, u32[]{:S(2)}) collective-permute-start(bf16[256,1024]{1,0:T(8,128)(2,1)S(1)} %collective-permute-done.1), channel_id=1, source_target_pairs={{0,1},{1,0},{2,3},{3,2},{4,5},{5,4},{6,7},{7,6},{8,9},{9,8},{10,11... | collective-permute-start | bytes 1572872 | tf_op jit(solution)/shard_map/gather_hidden/ppermute | solution.py:532
  36.1 15.5 %collective-permute-start.4 = (bf16[256,1024]{1,0:T(8,128)(2,1)S(1)}, bf16[256,1024]{1,0:T(8,128)(2,1)S(1)}, u32[]{:S(2)}, u32[]{:S(2)}) collective-permute-start(bf16[256,1024]{1,0:T(8,128)(2,1)S(1)} %collective-permute-done.3), channel_id=1, source_target_pairs={{0,1},{1,0},{2,3},{3,2},{4,5},{5,4},{6,7},{7,6},{8,9},{9,8},{10,11... | collective-permute-start | bytes 1572872 | tf_op jit(solution)/shard_map/gather_hidden/ppermute | solution.py:532
  50.9 38.8 %collective-permute-start.21 = (bf16[256,1024]{1,0:T(8,128)(2,1)}, bf16[256,1024]{1,0:T(8,128)(2,1)}, u32[]{:S(2)}, u32[]{:S(2)}) collective-permute-start(bf16[256,1024]{1,0:T(8,128)(2,1)} %get-tuple-element.59), channel_id=1, source_target_pairs={{0,2},{1,5},{2,0},{3,7},{4,6},{5,1},{6,4},{7,3},{8,10},{9,13},{10,... | collective-permute-start | bytes 1572872 | tf_op jit(solution)/shard_map/gather_cotangent/ppermute | solution.py:541
  89.2 40.0 %collective-permute-start.18 = (bf16[256,1024]{1,0:T(8,128)(2,1)}, bf16[256,1024]{1,0:T(8,128)(2,1)}, u32[]{:S(2)}, u32[]{:S(2)}) collective-permute-start(bf16[256,1024]{1,0:T(8,128)(2,1)} %collective-permute-done.17), channel_id=1, source_target_pairs={{0,1},{1,0},{2,3},{3,2},{4,5},{5,4},{6,7},{7,6},{8,9},{9,8},{10,11... | collective-permute-start | bytes 1572872 | tf_op jit(solution)/shard_map/gather_cotangent/ppermute | solution.py:532
  89.7 45.5 %collective-permute-start.20 = (bf16[256,1024]{1,0:T(8,128)(2,1)}, bf16[256,1024]{1,0:T(8,128)(2,1)}, u32[]{:S(2)}, u32[]{:S(2)}) collective-permute-start(bf16[256,1024]{1,0:T(8,128)(2,1)} %collective-permute-done.19), channel_id=1, source_target_pairs={{0,1},{1,0},{2,3},{3,2},{4,5},{5,4},{6,7},{7,6},{8,9},{9,8},{10,11... | collective-permute-start | bytes 1572872 | tf_op jit(solution)/shard_map/gather_cotangent/ppermute | solution.py:532
  89.7 85.5 %collective-permute-start.22 = (bf16[256,1024]{1,0:T(8,128)(2,1)}, bf16[256,1024]{1,0:T(8,128)(2,1)}, u32[]{:S(2)}, u32[]{:S(2)}) collective-permute-start(bf16[256,1024]{1,0:T(8,128)(2,1)} %collective-permute-done.21), channel_id=1, source_target_pairs={{0,1},{1,0},{2,3},{3,2},{4,5},{5,4},{6,7},{7,6},{8,9},{9,8},{10,11... | collective-permute-start | bytes 1572872 | tf_op jit(solution)/shard_map/gather_cotangent/ppermute | solution.py:532
  104.6 63.4 %collective-permute-start.10 = (bf16[256,1024]{1,0:T(8,128)(2,1)}, bf16[256,1024]{1,0:T(8,128)(2,1)}, u32[]{:S(2)}, u32[]{:S(2)}) collective-permute-start(bf16[256,1024]{1,0:T(8,128)(2,1)} %get-tuple-element.69), channel_id=1, source_target_pairs={{0,2},{1,3},{2,0},{3,1},{4,6},{5,7},{6,4},{7,5},{8,10},{9,11},{10,... | collective-permute-start | bytes 1572872 | tf_op jit(solution)/shard_map/gather_hidden_two/ppermute | solution.py:532
  106.1 59.5 %collective-permute-start.9 = (bf16[256,1024]{1,0:T(8,128)(2,1)}, bf16[256,1024]{1,0:T(8,128)(2,1)}, u32[]{:S(2)}, u32[]{:S(2)}) collective-permute-start(bf16[256,1024]{1,0:T(8,128)(2,1)} %get-tuple-element.69), channel_id=1, source_target_pairs={{0,1},{1,0},{2,3},{3,2},{4,5},{5,4},{6,7},{7,6},{8,9},{9,8},{10,11... | collective-permute-start | bytes 1572872 | tf_op jit(solution)/shard_map/gather_hidden_two/ppermute | solution.py:532
  129.1 105.5 %reduce-scatter.3.cloned.1.call-start = ((), (), s32[]{:S(2)}) async-start(), calls=%async_computation.8 | async-start | bytes 2359296 | tf_op jit(solution)/shard_map/grad_proj/reduce_scatter | solution.py:690
  129.1 38.9 %collective-permute-start.12 = (bf16[256,1024]{1,0:T(8,128)(2,1)}, bf16[256,1024]{1,0:T(8,128)(2,1)}, u32[]{:S(2)}, u32[]{:S(2)}) collective-permute-start(bf16[256,1024]{1,0:T(8,128)(2,1)} %get-tuple-element.69), channel_id=1, source_target_pairs={{0,4},{4,0},{1,5},{5,1},{2,6},{6,2},{3,7},{7,3},{8,12},{12,8},{9,1... | collective-permute-start | bytes 1572872 | tf_op jit(solution)/shard_map/gather_hidden_two/ppermute | solution.py:532
  185.2 26.2 %collective-permute-start.8 = (bf16[256,384]{1,0:T(8,128)(2,1)S(1)}, bf16[256,384]{1,0:T(8,128)(2,1)S(1)}, u32[]{:S(2)}, u32[]{:S(2)}) collective-permute-start(bf16[256,384]{1,0:T(8,128)(2,1)S(1)} %fusion.97), channel_id=1, source_target_pairs={{0,24},{8,16},{16,8},{24,0},{1,25},{9,17},{17,9},{25,1},{2,26},{10... | collective-permute-start | bytes 589832 | tf_op jit(solution)/shard_map/grad_qkv_weights/ppermute | solution.py:573
  202.4 15.5 %collective-permute-start.25 = (bf16[512,512]{1,0:T(8,128)(2,1)}, bf16[512,512]{1,0:T(8,128)(2,1)}, u32[]{:S(2)}, u32[]{:S(2)}) collective-permute-start(bf16[512,512]{1,0:T(8,128)(2,1)} %fusion.71), channel_id=1, source_target_pairs={{0,8},{8,0},{16,24},{24,16},{1,9},{9,1},{17,25},{25,17},{2,10},{10... | collective-permute-start | bytes 1572872 | tf_op jit(solution)/shard_map/grad_down/ppermute | solution.py:571
  209.3 15.5 %collective-permute-start.23 = (bf16[512,512]{1,0:T(8,128)(2,1)S(1)}, bf16[512,512]{1,0:T(8,128)(2,1)S(1)}, u32[]{:S(2)}, u32[]{:S(2)}) collective-permute-start(bf16[512,512]{1,0:T(8,128)(2,1)S(1)} %fusion.68), channel_id=1, source_target_pairs={{0,8},{8,0},{16,24},{24,16},{1,9},{9,1},{17,25},{25,17},{2,10},{10... | collective-permute-start | bytes 1572872 | tf_op jit(solution)/shard_map/grad_up/ppermute | solution.py:571
  214.0 20.6 %all-to-all-start.3 = ((bf16[8,32,384]{2,1,0:T(8,128)(2,1)}), bf16[8,32,384]{2,1,0:T(8,128)(2,1)S(1)}, u32[]{:S(2)}, u32[]{:S(2)}) async-start(bf16[8,32,384]{2,1,0:T(8,128)(2,1)} %bitcast.18), calls=%async_computation.3 | async-start | bytes 393216 | tf_op jit(solution)/shard_map/rows_exchange/all_to_all | solution.py:553
  217.9 43.5 %reduce-scatter.5.cloned.1.call-start = ((), (), s32[]{:S(2)}) async-start(), calls=%async_computation.9 | async-start | bytes 327680 | tf_op jit(solution)/shard_map/grad_proj/reduce_scatter | solution.py:693
  226.7 17.1 %collective-permute-start.24 = (bf16[256,512]{1,0:T(8,128)(2,1)S(1)}, bf16[256,512]{1,0:T(8,128)(2,1)S(1)}, u32[]{:S(2)}, u32[]{:S(2)}) collective-permute-start(bf16[256,512]{1,0:T(8,128)(2,1)S(1)} %fusion.92), channel_id=1, source_target_pairs={{0,24},{8,16},{16,8},{24,0},{1,25},{9,17},{17,9},{25,1},{2,26},{10... | collective-permute-start | bytes 786440 | tf_op jit(solution)/shard_map/grad_up/ppermute | solution.py:573
  234.6 15.3 %all-to-all-start.5 = ((bf16[8,32,512]{2,1,0:T(8,128)(2,1)}), bf16[8,32,512]{2,1,0:T(8,128)(2,1)S(1)}, u32[]{:S(2)}, u32[]{:S(2)}) async-start(bf16[8,32,512]{2,1,0:T(8,128)(2,1)} %bitcast.27), calls=%async_computation.7 | async-start | bytes 524288 | tf_op jit(solution)/shard_map/rows_exchange/all_to_all | solution.py:553
  253.3 103.9 %all-gather.3.cloned.1.call-start = ((), (), s32[]{:S(2)}) async-start(), calls=%async_computation.10 | async-start | bytes 3932160 | tf_op jit(solution)/shard_map/copies/all_gather | solution.py:763
  268.9 33.1 %all-to-all-start.2 = ((bf16[8,256,384]{1,2,0:T(8,128)(2,1)}), bf16[8,256,384]{1,2,0:T(8,128)(2,1)}, u32[]{:S(2)}, u32[]{:S(2)}) async-start(bf16[8,256,384]{1,2,0:T(8,128)(2,1)} %copy.54), calls=%async_computation.2 | async-start | bytes 3145728 | tf_op jit(solution)/shard_map/grad_qkv_exchange/all_to_all | solution.py:553
  (57 other events, 711.3 us)
Sparse Core Ops, SparseCore 0:
  179.6 39.9 reduce-scatter.2
  234.7 26.6 reduce-scatter.4
  267.4 44.4 all-gather.2
